TPU v7x, 128 devices: a whole 4x4x4 slice. The times are simulated.
128 devices in a mesh: tm: 128 (over z, y, x, core).
Axes of the slice: x: 4, y: 4, z: 4, core: 2. Of those that a mesh axis runs over, the one named last changes fastest.
Arguments:
- hidden: bfloat16 [49152, 8192], P('tm'), may hold values from -6 to 6
- norm_gain: float32 [8192], replicated, may hold values from 0.1 to 1.9
- w_in: bfloat16 [8192, 768], replicated, may hold values from -0.0625 to 0.0625
- w_short: float32 [768, 7], replicated, may hold values from -2 to 2
- residues: float32 [8, 16], replicated, may hold values from -4 to 4
- rates: float32 [8, 16], replicated, may hold values from 4.06901042e-06 to 0.0333333333, as said below
- skip: float32 [256], replicated, may hold values from -4 to 4
- w_out: bfloat16 [256, 8192], replicated, may hold values from -0.375 to 0.375
Outputs:
- mixed: bfloat16 [49152, 8192], P('tm')
Inputs may be any that keep to these rules, and one draw needn't show every extreme that they name: `rates`: every rate is positive.
All inputs are finite; a program needn't handle non-finite values.
Results may differ from a plain program's by a relative error of at most 0.0088.
Values may be sent and summed in bfloat16 or wider, within the bound.
No kernel may reach another device: no remote copies, remote signals or barrier semaphores. Data moves between devices by JAX's collectives and lax.ppermute only.
A program may use at most 256 MiB of HBM per device.

v0:
```python
import jax
import jax.numpy as jnp
from jax import lax
from jax.sharding import PartitionSpec as P

HIGHEST = lax.Precision.HIGHEST


def shifted(block, axis, distance):
    devices = range(lax.axis_size(axis))
    route = [(i - distance, i) for i in devices if i - distance in devices]
    return lax.ppermute(block, axis, route)


def own_block(fragment, tok_rows, rates, residues):
    weights = residues * jnp.sqrt(2.0 * rates)
    steps_idx = jnp.arange(tok_rows, dtype=jnp.int32)
    lag_matrix = (steps_idx[None, :] - steps_idx[:, None]).astype(jnp.float32)
    decays = jnp.exp(-rates[:, :, None, None] * jnp.maximum(lag_matrix, 0.0)[None, None, :, :])
    toeplitz = jnp.einsum("gm,gmst->gst", weights, decays, precision=HIGHEST)
    toeplitz = jnp.where((lag_matrix >= 0.0)[None, :, :], toeplitz, 0.0)
    return jnp.einsum(
        "gcs,gst->gct", fragment, toeplitz, precision=HIGHEST, preferred_element_type=jnp.float32
    )


def on_device(hidden, norm_gain, w_in, w_short, residues, rates, skip, w_out):
    tok_rows = hidden.shape[0]
    chan_total = w_short.shape[0] // 3
    group_count = rates.shape[0]
    chan_group = chan_total // group_count
    tap_count = w_short.shape[1]
    own_start = lax.axis_index("tm") * tok_rows
    widened = hidden.astype(jnp.float32)
    inv_scale = lax.rsqrt(jnp.mean(widened * widened, axis=1, keepdims=True) + 1e-06)
    normed = (widened * inv_scale * norm_gain).astype(jnp.bfloat16)
    projected = lax.dot_general(
        w_in, normed, (((0,), (1,)), ((), ())), preferred_element_type=jnp.float32
    ).astype(jnp.bfloat16)
    edge_cols = shifted(projected[:, tok_rows - (tap_count - 1) :], "tm", 1)
    extended = jnp.concatenate([edge_cols, projected], axis=1).astype(jnp.float32)
    features = jnp.zeros(projected.shape, jnp.float32)
    for offset_tap in range(tap_count):
        begin = tap_count - 1 - offset_tap
        features = (
            features
            + w_short[:, offset_tap : offset_tap + 1] * extended[:, begin : begin + tok_rows]
        )
    queries = features[:chan_total]
    keyed = features[chan_total : 2 * chan_total]
    valued = features[2 * chan_total :]
    product = (keyed * valued).astype(jnp.bfloat16)
    product_wide = product.astype(jnp.float32).reshape(group_count, chan_group, tok_rows)
    local_part = own_block(product_wide, tok_rows, rates, residues)
    positions = jnp.arange(tok_rows, dtype=jnp.float32)
    fragment = lax.all_gather(product, "tm", axis=1, tiled=True)
    width = fragment.shape[1]
    spots = jnp.arange(width, dtype=jnp.int32)
    distance = (own_start - 1 - spots).astype(jnp.float32)
    factor = jnp.exp(-rates[:, None, :] * jnp.maximum(distance, 0.0)[None, :, None])
    factor = jnp.where((spots < own_start)[None, :, None], factor, 0.0)
    grouped = fragment.astype(jnp.float32).reshape(group_count, chan_group, width)
    states = jnp.einsum(
        "gcw,gwm->gcm", grouped, factor, precision=HIGHEST, preferred_element_type=jnp.float32
    )
    weights = residues * jnp.sqrt(2.0 * rates)
    rising = jnp.exp(-rates[:, :, None] * (positions + 1.0)[None, None, :])
    convolved = local_part + jnp.einsum(
        "gcm,gmt->gct",
        states * weights[:, None, :],
        rising,
        precision=HIGHEST,
        preferred_element_type=jnp.float32,
    )
    convolved = convolved.reshape(chan_total, tok_rows)
    product_flat = product_wide.reshape(chan_total, tok_rows)
    gated = (queries * (convolved + skip[:, None] * product_flat)).astype(jnp.bfloat16)
    mixed = lax.dot_general(
        gated, w_out, (((0,), (0,)), ((), ())), preferred_element_type=jnp.float32
    )
    return mixed.astype(jnp.bfloat16)


def solution(mesh):
    return jax.shard_map(
        on_device,
        mesh=mesh,
        in_specs=(P("tm", None), P(), P(), P(), P(), P(), P(), P()),
        out_specs=P("tm", None),
        check_vma=False,
    )
```

profile of v0, /device:TPU:32, one launch (start us, length us, event | category | flops | bytes accessed | tf_op | source)
XLA Modules:
  0.0 230.6 jit_solution(6560298311716021537)
XLA Ops:
  6.5 4.3 %fusion.6 = f32[384]{0:T(512)S(1)} fusion(bf16[384,8192]{1,0:T(8,128)(2,1)} %param.8), kind=kLoop, calls=%fused_computation.9 | loop fusion | flops 9436800 | bytes 6292992 | tf_op jit(solution)/shard_map/reduce_sum | solution.py:35
  10.8 0.3 copy-done
  11.1 8.3 %fusion.24 = bf16[768,384]{0,1:T(8,128)(2,1)S(1)} fusion(bf16[8192,768]{1,0:T(8,128)(2,1)} %param.10, bf16[384,8192]{1,0:T(8,128)(2,1)S(1)} %copy-done, f32[8192]{0:T(1024)} %param.9, f32[384]{0:T(512)S(1)} %add_rsqrt_fusion), kind=kOutput, calls=%fused_computation.26 | convolution fusion | flops 4844716032 | bytes 19498496 | tf_op jit(solution)/shard_map/dot_general | solution.py:37
  19.5 1.9 collective-permute-start
  21.4 0.1 slice_reduce_fusion.6
  21.5 7.2 %collective-permute-done = bf16[768,6]{0,1:T(8,128)(2,1)S(1)} collective-permute-done((bf16[768,6]{0,1:T(8,128)(2,1)S(1)}, bf16[768,6]{0,1:T(8,128)(2,1)S(1)}, u32[]{:S(2)}, u32[]{:S(2)}) %collective-permute-start) | collective-permute-done | bytes 9248 | tf_op jit(solution)/shard_map/ppermute | solution.py:12
  28.7 0.1 maximum_convert_fusion
  28.8 0.0 copy-start.4
  28.8 0.0 copy-start.5
  28.9 1.0 fusion.27
  29.8 0.7 fusion.36
  30.5 0.0 all-gather.2.cloned.1.call-update
  30.6 0.1 convert_compare_fusion
  30.7 0.1 convert_maximum_fusion
  30.9 24.4 %multiply_exponential_fusion = f32[8,16,384,384]{3,2,1,0:T(8,128)} fusion(f32[384,384]{1,0:T(8,128)S(1)} %convert_maximum_fusion, f32[8,16]{1,0:T(8,128)S(1)} %get-tuple-element.12), kind=kLoop, calls=%fused_computation.2 | loop fusion | flops 18874368 | bytes 76087808 | tf_op jit(solution)/shard_map/exp | solution.py:19
  55.3 98.0 %fusion = f32[8,1,384,384]{3,1,2,0:T(1,128)} fusion(f32[8,16,1,1]{1,2,3,0:T(1,128)S(1)} %bitcast.20, f32[8,16,384,384]{3,2,1,0:T(8,128)} %multiply_exponential_fusion), kind=kOutput, calls=%fused_computation | convolution fusion | flops 226492416 | bytes 80216576 | tf_op jit(solution)/shard_map/gm,gmst->gst/dot_general | solution.py:20
  153.4 0.2 copy.14
  153.5 4.4 %fusion.17 = f32[8,32,384]{2,1,0:T(8,128)S(1)} fusion(bf16[8,32,384]{2,1,0:T(8,128)(2,1)S(1)} %bitcast.19, f32[8,1,384,384]{3,1,2,0:T(1,128)} %fusion, pred[384,384]{1,0:T(8,128)(4,1)S(1)} %convert_compare_fusion), kind=kOutput, calls=%fused_computation.21 | convolution fusion | flops 454164480 | bytes 5455872 | tf_op jit(solution)/shard_map/gcs,gst->gct/dot_general | solution.py:22
  157.9 0.0 all-gather.2.cloned.1.call-done
  157.9 32.7 %copy.15 = bf16[256,49152]{1,0:T(8,128)(2,1)} copy(bf16[256,49152]{0,1:T(8,128)(2,1)} %all-gather.2.cloned.1.call-done) | data formatting | bytes 50331648 | tf_op jit(solution)/shard_map/all_gather | solution.py:56
  190.6 25.6 %fusion.33 = f32[8,32,16]{1,2,0:T(8,128)S(1)} fusion(bf16[8,32,49152]{2,1,0:T(8,128)(2,1)} %bitcast.17, f32[49152]{0:T(1024)S(1)} %convert_maximum_fusion.1, f32[8,16]{1,0:T(8,128)S(1)} %get-tuple-element.12, pred[49152]{0:T(1024)(128)(4,1)S(1)} %iota_compare_fusion, f32[8,16]{1,0:T(8,128)S(1)} %get-tuple-element.13), kind=kOutput, calls=%fused_computation.41 | convolution fusion | flops 2428506112 | bytes 25428992 | tf_op jit(solution)/shard_map/gcw,gwm->gcm/dot_general | solution.py:63
  216.3 0.6 convolution_add_fusion
  216.9 0.2 copy.16
  217.1 6.7 %convolution_convert_fusion = bf16[384,8192]{1,0:T(8,128)(2,1)} fusion(bf16[256,8192]{1,0:T(8,128)(2,1)} %param.15, f32[768,384]{0,1:T(8,128)S(1)} %fusion.27, f32[256,384]{0,1:T(8,128)S(1)} %copy.16, bf16[256,384]{0,1:T(8,128)(2,1)S(1)} %copy-done.1, f32[256]{0:T(256)S(1)} %copy-done.3), kind=kOutput, calls=%fused_computation.16 | convolution fusion | flops 1614249984 | bytes 11469824 | tf_op jit(solution)/shard_map/dot_general | solution.py:78
  (16 shorter events, 0.1 us)
Async XLA Ops:
  6.5 151.4 %all-gather.2.cloned.1.call-start = ((), (), s32[]{:S(2)}) async-start(), calls=%async_computation | async-start | bytes 25362432 | tf_op jit(solution)/shard_map/all_gather | solution.py:56
  6.5 4.6 %copy-start = (bf16[384,8192]{1,0:T(8,128)(2,1)S(1)}, bf16[384,8192]{1,0:T(8,128)(2,1)}, u32[]{:S(2)}) copy-start(bf16[384,8192]{1,0:T(8,128)(2,1)} %param.8) | copy-start | bytes 18874372
  11.1 10.3 %copy-start.2 = (f32[768,7]{0,1:T(8,128)S(1)}, f32[768,7]{0,1:T(8,128)}, u32[]{:S(2)}) copy-start(f32[768,7]{0,1:T(8,128)} %param.11) | copy-start | bytes 64516
  19.5 9.2 %collective-permute-start = (bf16[768,6]{0,1:T(8,128)(2,1)S(1)}, bf16[768,6]{0,1:T(8,128)(2,1)S(1)}, u32[]{:S(2)}, u32[]{:S(2)}) collective-permute-start(bf16[768,6]{0,1:T(8,128)(2,1)S(1)} %slice.72), channel_id=1, source_target_pairs={{0,1},{1,2},{2,3},{3,4},{4,5},{5,6},{6,7},{7,8},{8,9},{9,10},{10,1... | collective-permute-start | bytes 27656 | tf_op jit(solution)/shard_map/ppermute | solution.py:12
  28.8 2.0 copy-start.4
  28.8 2.0 copy-start.5
  55.3 98.0 %copy-start.1 = (bf16[256,384]{0,1:T(8,128)(2,1)S(1)}, bf16[256,384]{0,1:T(8,128)(2,1)}, u32[]{:S(2)}) copy-start(bf16[256,384]{0,1:T(8,128)(2,1)} %fusion.36) | copy-start | bytes 589828
  190.6 26.4 %copy-start.3 = (f32[256]{0:T(256)S(1)}, f32[256]{0:T(256)}, u32[]{:S(2)}) copy-start(f32[256]{0:T(256)} %param.14) | copy-start | bytes 3076
Sparse Core Ops, SparseCore 0:
  30.7 90.2 all-gather.1
where the time goes:
time: 232 us; the launch traced here: 231 us
  matrix products  144 us (62%)
  local copies, waits for them, and re-layouts  33.5 us (14%)
  other arithmetic  30.8 us (13%)
  between operations  13.6 us (6%)
  waiting for transfers between devices  7.26 us (3%)
    dot_general x1, matrix products, own_block(): toeplitz = jnp.einsum('gm,gmst->gst', weights, decays, precision=HIGHEST)  98 us
    all_gather x1, local copies, waits for them, and re-layouts, on_device(): fragment = lax.all_gather(product, 'tm', axis=1, tiled=True)  32.7 us
    dot_general x1, matrix products, on_device(): jnp.einsum('gcw,gwm->gcm', grouped, factor, precision=HIGHEST, preferred_...  25.6 us
    exp x1, other arithmetic, own_block(): jnp.exp(-rates[:, :, None, None] * jnp.maximum(lag_matrix, 0.0)[None, Non...  24.4 us
    dot_general x1, matrix products, on_device(): lax.dot_general(w_in, normed, (((0,), (1,)), ((), ())), preferred_element...  8.31 us
    ppermute x1, waiting for transfers between devices, shifted(): return lax.ppermute(block, axis, route)  7.22 us
    dot_general x1, matrix products, on_device(): lax.dot_general(gated, w_out, (((0,), (0,)), ((), ())), preferred_element...  6.7 us
  transfers between devices with their start and end apart: 2, of which 1 were waited for; matrix products, arithmetic and copies ran while one was open for 55% of the time, Pallas kernels for 0%

commit v1 on v0

--- a/solution.py
+++ b/solution.py
@@ -53,7 +53,9 @@
     product_wide = product.astype(jnp.float32).reshape(group_count, chan_group, tok_rows)
     local_part = own_block(product_wide, tok_rows, rates, residues)
     positions = jnp.arange(tok_rows, dtype=jnp.float32)
-    fragment = lax.all_gather(product, "tm", axis=1, tiled=True)
+    fragment = jnp.concatenate(
+        lax.all_to_all(jnp.stack([product] * lax.axis_size("tm")), "tm", 0, 0), axis=1
+    )
     width = fragment.shape[1]
     spots = jnp.arange(width, dtype=jnp.int32)
     distance = (own_start - 1 - spots).astype(jnp.float32)

time: 232 us -> 527 us (2.27)
  the two profiles are of different devices: /device:TPU:32 before, /device:TPU:2 now
where the time goes in v1:
time: 527 us; the launch traced here: 526 us
  waiting for transfers between devices  274 us (52%)
  matrix products  141 us (27%)
  local copies, waits for them, and re-layouts  68.2 us (13%)
  other arithmetic  30 us (6%)
  starting transfers between devices  12.9 us (2%)
    all_to_all x1, waiting for transfers between devices, on_device(): lax.all_to_all(jnp.stack([product] * lax.axis_size('tm')), 'tm', 0, 0)  271 us
    dot_general x1, matrix products, own_block(): toeplitz = jnp.einsum('gm,gmst->gst', weights, decays, precision=HIGHEST)  97.4 us
    reshape x1, local copies, waits for them, and re-layouts, on_device(): fragment.astype(jnp.float32).reshape(group_count, chan_group, width)  31.2 us
    reshape x1, local copies, waits for them, and re-layouts, on_device(): jnp.concatenate(lax.all_to_all(jnp.stack([product] * lax.axis_size('tm'))...  27 us
    dot_general x1, matrix products, on_device(): jnp.einsum('gcw,gwm->gcm', grouped, factor, precision=HIGHEST, preferred_...  25.6 us
    exp x1, other arithmetic, own_block(): jnp.exp(-rates[:, :, None, None] * jnp.maximum(lag_matrix, 0.0)[None, Non...  24.4 us
    all_to_all x1, starting transfers between devices, on_device(): lax.all_to_all(jnp.stack([product] * lax.axis_size('tm')), 'tm', 0, 0)  10.9 us
  transfers between devices with their start and end apart: 2, of which 2 were waited for; matrix products, arithmetic and copies ran while one was open for 24% of the time, Pallas kernels for 0%

profile of v1, /device:TPU:2, one launch (start us, length us, event | category | flops | bytes accessed | tf_op | source)
XLA Modules:
  0.0 525.7 jit_solution(1991268591618131894)
XLA Ops:
  0.0 4.3 fusion.6
  4.3 0.3 copy-done
  4.6 8.3 %fusion.24 = bf16[768,384]{0,1:T(8,128)(2,1)S(1)} fusion(bf16[8192,768]{1,0:T(8,128)(2,1)} %param.10, bf16[384,8192]{1,0:T(8,128)(2,1)S(1)} %copy-done, f32[8192]{0:T(1024)} %param.9, f32[384]{0:T(512)S(1)} %add_rsqrt_fusion), kind=kOutput, calls=%fused_computation.26 | convolution fusion | flops 4844716032 | bytes 19498496 | tf_op jit(solution)/shard_map/dot_general | solution.py:37
  12.9 1.9 collective-permute-start
  14.9 0.1 slice_reduce_fusion.6
  14.9 3.0 collective-permute-done
  17.9 0.1 maximum_convert_fusion
  18.1 1.0 fusion.27
  19.1 0.2 copy.15
  19.3 9.2 %stack.2 = bf16[128,256,384]{2,1,0:T(8,128)(2,1)} broadcast(bf16[256,384]{1,0:T(8,128)(2,1)S(1)} %copy.15), dimensions={1,2} | broadcast | bytes 25362432 | tf_op jit(solution)/shard_map/stack | solution.py:57
  28.5 10.9 %all-to-all-start = ((bf16[128,256,384]{2,1,0:T(8,128)(2,1)}), bf16[128,256,384]{2,1,0:T(8,128)(2,1)}, u32[]{:S(2)}, u32[]{:S(2)}) async-start(bf16[128,256,384]{2,1,0:T(8,128)(2,1)} %stack.2), calls=%async_computation | async-start | bytes 50331648 | tf_op jit(solution)/shard_map/all_to_all | solution.py:57
  39.4 0.1 convert_compare_fusion
  39.6 0.1 convert_maximum_fusion
  39.7 0.0 copy-done.3
  39.8 24.4 %multiply_exponential_fusion = f32[8,16,384,384]{3,2,1,0:T(8,128)} fusion(f32[384,384]{1,0:T(8,128)S(1)} %convert_maximum_fusion, f32[8,16]{1,0:T(8,128)S(1)} %get-tuple-element.12), kind=kLoop, calls=%fused_computation.2 | loop fusion | flops 18874368 | bytes 76087808 | tf_op jit(solution)/shard_map/exp | solution.py:19
  64.1 97.4 %fusion = f32[8,1,384,384]{3,1,2,0:T(1,128)S(1)} fusion(f32[8,16,1,1]{1,2,3,0:T(1,128)S(1)} %bitcast.19, f32[8,16,384,384]{3,2,1,0:T(8,128)} %multiply_exponential_fusion), kind=kOutput, calls=%fused_computation | convolution fusion | flops 226492416 | bytes 80216576 | tf_op jit(solution)/shard_map/gm,gmst->gst/dot_general | solution.py:20
  161.5 2.1 fusion.17
  163.7 270.7 %all-to-all-done = bf16[128,256,384]{2,1,0:T(8,128)(2,1)} async-done(((bf16[128,256,384]{2,1,0:T(8,128)(2,1)}), bf16[128,256,384]{2,1,0:T(8,128)(2,1)}, u32[]{:S(2)}, u32[]{:S(2)}) %all-to-all-start) | async-done | bytes 25165856 | tf_op jit(solution)/shard_map/all_to_all | solution.py:57
  434.3 27.0 %copy.17 = bf16[256,128,384]{2,1,0:T(8,128)(2,1)} copy(bf16[256,128,384]{2,0,1:T(8,128)(2,1)} %bitcast.5) | data formatting | bytes 50331648 | tf_op jit(solution)/shard_map/reshape | solution.py:56
  461.3 31.2 %reshape.77 = bf16[8,32,49152]{2,1,0:T(8,128)(2,1)} reshape(bf16[256,128,384]{2,1,0:T(8,128)(2,1)} %copy.17) | data formatting | bytes 50331648 | tf_op jit(solution)/shard_map/reshape | solution.py:64
  492.6 25.6 %fusion.33 = f32[8,32,16]{1,2,0:T(8,128)S(1)} fusion(bf16[8,32,49152]{2,1,0:T(8,128)(2,1)} %reshape.77, f32[49152]{0:T(1024)S(1)} %convert_maximum_fusion.1, f32[8,16]{1,0:T(8,128)S(1)} %get-tuple-element.12, pred[49152]{0:T(1024)(128)(4,1)S(1)} %iota_compare_fusion, f32[8,16]{1,0:T(8,128)S(1)} %get-tuple-element.13), kind=kOutput, calls=%fused_computation.41 | convolution fusion | flops 2428506112 | bytes 25428992 | tf_op jit(solution)/shard_map/gcw,gwm->gcm/dot_general | solution.py:65
  518.2 0.6 convolution_add_fusion
  518.8 0.2 copy.18
  519.0 6.7 %convolution_convert_fusion = bf16[384,8192]{1,0:T(8,128)(2,1)} fusion(bf16[256,8192]{1,0:T(8,128)(2,1)} %param.15, f32[768,384]{0,1:T(8,128)S(1)} %fusion.27, f32[256,384]{0,1:T(8,128)S(1)} %copy.18, bf16[256,384]{0,1:T(8,128)(2,1)S(1)} %fusion.36, f32[256]{0:T(256)S(1)} %copy-done.2), kind=kOutput, calls=%fused_computation.16 | convolution fusion | flops 1614249984 | bytes 11469824 | tf_op jit(solution)/shard_map/dot_general | solution.py:80
  (15 shorter events, 0.2 us)
Async XLA Ops:
  0.0 4.6 copy-start
  4.6 10.3 %copy-start.1 = (f32[768,7]{0,1:T(8,128)S(1)}, f32[768,7]{0,1:T(8,128)}, u32[]{:S(2)}) copy-start(f32[768,7]{0,1:T(8,128)} %param.11) | copy-start | bytes 64516
  12.9 5.0 collective-permute-start
  28.5 11.2 %copy-start.3 = (f32[8,16]{1,0:T(8,128)S(1)}, f32[8,16]{1,0:T(8,128)}, u32[]{:S(2)}) copy-start(f32[8,16]{1,0:T(8,128)} %param.13) | copy-start | bytes 1540
  28.5 11.2 %copy-start.4 = (f32[8,16]{1,0:T(8,128)S(1)}, f32[8,16]{1,0:T(8,128)}, u32[]{:S(2)}) copy-start(f32[8,16]{1,0:T(8,128)} %param.12) | copy-start | bytes 1540
  28.5 405.8 %all-to-all-start = ((bf16[128,256,384]{2,1,0:T(8,128)(2,1)}), bf16[128,256,384]{2,1,0:T(8,128)(2,1)}, u32[]{:S(2)}, u32[]{:S(2)}) async-start(bf16[128,256,384]{2,1,0:T(8,128)(2,1)} %stack.2), calls=%async_computation | async-start | bytes 50331648 | tf_op jit(solution)/shard_map/all_to_all | solution.py:57
  492.6 26.4 %copy-start.2 = (f32[256]{0:T(256)S(1)}, f32[256]{0:T(256)}, u32[]{:S(2)}) copy-start(f32[256]{0:T(256)} %param.14) | copy-start | bytes 3076
